TPU v7x, 32 devices: a whole 2x2x4 slice. The times are simulated.
32 devices in a mesh: dp: 8 (over y, x, core), seq: 4 (over z).
Axes of the slice: x: 2, y: 2, z: 4, core: 2. Of those that a mesh axis runs over, the one named last changes fastest.
Arguments:
- tokens: bfloat16 [2, 8, 1024, 1600], P(None, 'dp', 'seq'), may hold values from -6 to 6
- doc_ids: int32 [2, 8, 1024], P(None, 'dp', 'seq'), may hold values from 0 to 15, never falling along the last dimension, each value on 1 to 256 neighbouring positions
- cotangent: bfloat16 [2, 8, 1024, 1600], P(None, 'dp', 'seq'), may hold values from -6 to 6
- enc_in: bfloat16 [1280000], P(('dp', 'seq')), may hold values from -0.15625 to 0.15625
- enc_conv: bfloat16 [3200000], P(('dp', 'seq')), may hold values from -0.09375 to 0.09375
- enc_out: bfloat16 [1280000], P(('dp', 'seq')), may hold values from -0.21875 to 0.21875
- enc_gain: float32 [3200], replicated, may hold values from 0.25 to 1.75
- enc_shift: float32 [3200], replicated, may hold values from -3 to 3
- enc_bias: float32 [1600], replicated, may hold values from -3 to 3
- dec_in: bfloat16 [1280000], P(('dp', 'seq')), may hold values from -0.15625 to 0.15625
- dec_conv: bfloat16 [1920000], P(('dp', 'seq')), may hold values from -0.125 to 0.125
- dec_out: bfloat16 [1280000], P(('dp', 'seq')), may hold values from -0.21875 to 0.21875
- dec_gain: float32 [3200], replicated, may hold values from 0.25 to 1.75
- dec_shift: float32 [3200], replicated, may hold values from -3 to 3
- dec_bias: float32 [1600], replicated, may hold values from -3 to 3
Outputs:
- output: bfloat16 [2, 8, 1024, 1600], P(None, 'dp', 'seq')
- token_grad: float32 [2, 8, 1024, 1600], P(None, 'dp', 'seq')
- enc_in_grad: float32 [1280000], P(('dp', 'seq'))
- enc_conv_grad: float32 [3200000], P(('dp', 'seq'))
- enc_out_grad: float32 [1280000], P(('dp', 'seq'))
- enc_gain_grad: float32 [3200], replicated
- enc_shift_grad: float32 [3200], replicated
- enc_bias_grad: float32 [1600], replicated
- dec_in_grad: float32 [1280000], P(('dp', 'seq'))
- dec_conv_grad: float32 [1920000], P(('dp', 'seq'))
- dec_out_grad: float32 [1280000], P(('dp', 'seq'))
- dec_gain_grad: float32 [3200], replicated
- dec_shift_grad: float32 [3200], replicated
- dec_bias_grad: float32 [1600], replicated
Inputs may be any that keep to these rules, and one draw needn't show every extreme that they name: `doc_ids`: along each sequence the document numbers never fall; each document has 1 to 256 characters.
All inputs are finite; a program needn't handle non-finite values.
Results may differ from a plain program's by a relative error of at most 0.012.
Values may be sent and summed in bfloat16 or wider, within the bound.
A program may use at most 192 MiB of HBM per device.

v0:
```python
import jax
import jax.numpy as jnp
from jax import lax
from jax.sharding import PartitionSpec as P

D2 = 1600
D = 800
ENCODER_TAPS = 5
ENCODER_SPACING = 4
DECODER_TAPS = 3
DECODER_SPACING = 8


epsilon = 1e-05


def from_behind(value, axis, by):
    length = lax.axis_size(axis)
    pairs = [(i, i + by) for i in range(length) if 0 <= i + by < length]
    return lax.ppermute(value, axis, pairs)


def extended(value, sides, width):
    for axis, dim in sides:
        size, length = (lax.axis_size(axis), value.shape[dim])
        up = [(i, (i + 1) % size) for i in range(size - 1)]
        down = [(j, i) for i, j in up]
        last = lax.slice_in_dim(value, length - width, length, axis=dim)
        initial = lax.slice_in_dim(value, 0, width, axis=dim)
        before = lax.ppermute(last, axis, up)
        after = lax.ppermute(initial, axis, down)
        value = jnp.concatenate([before, value, after], axis=dim)
    return value


def normalize(values):
    centred = values - jnp.mean(values, axis=-1, keepdims=True)
    factor = lax.rsqrt(jnp.mean(centred * centred, axis=-1, keepdims=True) + epsilon)
    return (centred * factor, factor)


def silu_slope(hidden):
    sigma = jax.nn.sigmoid(hidden)
    return sigma * (1.0 + hidden * (1.0 - sigma))


def norm_back(grad_h, scale_row, normed, factor):
    scaled = grad_h * scale_row
    mean_one = jnp.mean(scaled, axis=-1, keepdims=True)
    mean_two = jnp.mean(scaled * normed, axis=-1, keepdims=True)
    grad_in = factor * (scaled - mean_one - normed * mean_two)
    return (grad_in, jnp.sum(grad_h * normed, axis=0), jnp.sum(grad_h, axis=0))


def tap_offsets(causal):
    if causal:
        return [
            DECODER_SPACING * (tap_position - DECODER_TAPS + 1)
            for tap_position in range(DECODER_TAPS)
        ]
    return [
        ENCODER_SPACING * (tap_position - (ENCODER_TAPS - 1) // 2)
        for tap_position in range(ENCODER_TAPS)
    ]


def stacked_taps(padded, lead_rows, seg_pad, segment_leading, shift_offsets, length):
    own_ids = seg_pad[:, segment_leading : segment_leading + length]
    pieces = []
    for offset in shift_offsets:
        shifted = padded[:, lead_rows + offset : lead_rows + offset + length]
        same_doc = (
            seg_pad[:, segment_leading + offset : segment_leading + offset + length] == own_ids
        )
        pieces.append(jnp.where(same_doc[:, :, None], shifted, jnp.zeros_like(shifted)))
    return jnp.concatenate(pieces, axis=-1)


def shape_weights(flat_three):
    return (
        flat_three[0].reshape(D2, D),
        flat_three[1].reshape(-1, D),
        flat_three[2].reshape(D, D2),
    )


def fetch_forward(input_weight, convolution_weight, output_weight):
    return shape_weights(
        (
            lax.all_gather(input_weight, ("dp", "seq"), axis=0, tiled=True),
            lax.all_gather(convolution_weight, ("dp", "seq"), axis=0, tiled=True),
            lax.all_gather(output_weight, ("dp", "seq"), axis=0, tiled=True),
        )
    )


def fetch_backward(input_weight, convolution_weight, output_weight):
    return shape_weights(
        (
            lax.all_gather(input_weight, ("dp", "seq"), axis=0, tiled=True),
            lax.all_gather(convolution_weight, ("dp", "seq"), axis=0, tiled=True),
            lax.all_gather(output_weight, ("dp", "seq"), axis=0, tiled=True),
        )
    )


def block_forward(
    inputs, seg_pad, segment_leading, weights, norm_gain, norm_shift, output_bias, causal
):
    input_weight, convolution_weight, output_weight = weights
    seqs_here, length, wide_dim = inputs.shape
    narrow = input_weight.shape[1]
    flat_rows = inputs.reshape(-1, wide_dim)
    normed_one, factor_one = normalize(flat_rows)
    hidden_one = normed_one * norm_gain[:wide_dim] + norm_shift[:wide_dim]
    act_first = jax.nn.silu(hidden_one).astype(jnp.bfloat16)
    narrowed_rows = jnp.dot(act_first, input_weight, preferred_element_type=jnp.float32)
    normed_two, factor_two = normalize(narrowed_rows)
    hidden_two = (
        normed_two * norm_gain[wide_dim : wide_dim + narrow]
        + norm_shift[wide_dim : wide_dim + narrow]
    )
    act_second = jax.nn.silu(hidden_two).astype(jnp.bfloat16).reshape(seqs_here, length, narrow)
    shift_offsets = tap_offsets(causal)
    reach_rows = max([abs(offset) for offset in shift_offsets])
    if causal:
        tail_rows = from_behind(act_second[:, length - reach_rows :], "seq", 1)
        padded = jnp.concatenate([tail_rows, act_second], axis=1)
    else:
        padded = extended(act_second, (("seq", 1),), reach_rows)
    stacked = stacked_taps(
        padded, reach_rows, seg_pad, segment_leading, shift_offsets, length
    ).reshape(flat_rows.shape[0], -1)
    convolved_output = jnp.dot(stacked, convolution_weight, preferred_element_type=jnp.float32)
    normed_three, factor_three = normalize(convolved_output)
    hidden_three = normed_three * norm_gain[wide_dim + narrow :] + norm_shift[wide_dim + narrow :]
    act_third = jax.nn.silu(hidden_three).astype(jnp.bfloat16)
    residual_branch = (
        jnp.dot(act_third, output_weight, preferred_element_type=jnp.float32) + output_bias
    )
    result = (flat_rows + residual_branch).reshape(inputs.shape)
    kept_state = (
        normed_one,
        factor_one,
        hidden_one,
        act_first,
        normed_two,
        factor_two,
        hidden_two,
        stacked,
        normed_three,
        factor_three,
        hidden_three,
        act_third,
    )
    return (result, kept_state)


def block_backward(
    grad_out, kept_state, seg_pad, segment_leading, weights, norm_gain, causal, seqs_here, length
):
    input_weight, convolution_weight, output_weight = weights
    (
        normed_one,
        factor_one,
        hidden_one,
        act_first,
        normed_two,
        factor_two,
        hidden_two,
        stacked,
        normed_three,
        factor_three,
        hidden_three,
        act_third,
    ) = kept_state
    wide_dim = input_weight.shape[0]
    narrow = input_weight.shape[1]
    grad_low = grad_out.astype(jnp.bfloat16)
    grad_bias = jnp.sum(grad_low.astype(jnp.float32), axis=0)
    grad_w_out = jnp.einsum("nc,nd->cd", act_third, grad_low, preferred_element_type=jnp.float32)
    grad_act = jnp.einsum("nd,cd->nc", grad_low, output_weight, preferred_element_type=jnp.float32)
    grad_act = grad_act * silu_slope(hidden_three)
    grad_conv_out, gain_three, shift_three = norm_back(
        grad_act, norm_gain[wide_dim + narrow :], normed_three, factor_three
    )
    grad_conv_low = grad_conv_out.astype(jnp.bfloat16)
    grad_w_conv = jnp.einsum(
        "nc,nd->cd", stacked, grad_conv_low, preferred_element_type=jnp.float32
    )
    shift_offsets = tap_offsets(causal)
    reach_rows = max([abs(offset) for offset in shift_offsets])
    grad_grid = grad_conv_low.reshape(seqs_here, length, narrow)
    if causal:
        head_rows = from_behind(grad_grid[:, :reach_rows], "seq", -1)
        padded = jnp.concatenate([grad_grid, head_rows], axis=1)
        lead_rows = 0
    else:
        padded = extended(grad_grid, (("seq", 1),), reach_rows)
        lead_rows = reach_rows
    back_stack = stacked_taps(
        padded, lead_rows, seg_pad, segment_leading, [-offset for offset in shift_offsets], length
    )
    back_stack = back_stack.reshape(-1, len(shift_offsets), narrow)
    grad_act = jnp.einsum(
        "nkj,kij->ni",
        back_stack,
        convolution_weight.reshape(len(shift_offsets), narrow, narrow),
        preferred_element_type=jnp.float32,
    )
    grad_act = grad_act * silu_slope(hidden_two)
    grad_narrow, gain_two, shift_two = norm_back(
        grad_act, norm_gain[wide_dim : wide_dim + narrow], normed_two, factor_two
    )
    grad_narrow_low = grad_narrow.astype(jnp.bfloat16)
    grad_w_in = jnp.einsum(
        "nc,nd->cd", act_first, grad_narrow_low, preferred_element_type=jnp.float32
    )
    grad_act = jnp.einsum(
        "nd,cd->nc", grad_narrow_low, input_weight, preferred_element_type=jnp.float32
    )
    grad_act = grad_act * silu_slope(hidden_one)
    grad_flat, gain_one, shift_one = norm_back(
        grad_act, norm_gain[:wide_dim], normed_one, factor_one
    )
    grad_input = grad_out + grad_flat
    grad_gain = jnp.concatenate([gain_one, gain_two, gain_three])
    grad_shift = jnp.concatenate([shift_one, shift_two, shift_three])
    return (
        grad_input,
        (grad_w_in.reshape(-1), grad_w_conv.reshape(-1), grad_w_out.reshape(-1)),
        (grad_gain, grad_shift, grad_bias),
    )


def per_device(
    tokens,
    doc_ids,
    cotangent,
    enc_in,
    enc_conv,
    enc_out,
    enc_gain,
    enc_shift,
    enc_bias,
    dec_in,
    dec_conv,
    dec_out,
    dec_gain,
    dec_shift,
    dec_bias,
):
    micro_count, seqs_here, length, wide_dim = tokens.shape
    segment_leading = max(
        ENCODER_SPACING * ((ENCODER_TAPS - 1) // 2), DECODER_SPACING * (DECODER_TAPS - 1)
    )
    outputs = []
    grads_in = []
    weight_sums = None
    small_sums = None
    for batch_index in range(micro_count):
        seg_pad = extended(doc_ids[batch_index], (("seq", 1),), segment_leading)
        enc_weights = fetch_forward(enc_in, enc_conv, enc_out)
        start_rows = tokens[batch_index].astype(jnp.float32)
        middle, enc_kept = block_forward(
            start_rows, seg_pad, segment_leading, enc_weights, enc_gain, enc_shift, enc_bias, False
        )
        dec_weights = fetch_forward(dec_in, dec_conv, dec_out)
        final_rows, dec_kept = block_forward(
            middle, seg_pad, segment_leading, dec_weights, dec_gain, dec_shift, dec_bias, True
        )
        outputs.append(final_rows.astype(jnp.bfloat16))
        grad_final = cotangent[batch_index].astype(jnp.float32).reshape(-1, wide_dim)
        dec_weights = fetch_backward(dec_in, dec_conv, dec_out)
        grad_middle, dec_wgrads, dec_small = block_backward(
            grad_final,
            dec_kept,
            seg_pad,
            segment_leading,
            dec_weights,
            dec_gain,
            True,
            seqs_here,
            length,
        )
        enc_weights = fetch_backward(enc_in, enc_conv, enc_out)
        grad_start, enc_wgrads, enc_small = block_backward(
            grad_middle,
            enc_kept,
            seg_pad,
            segment_leading,
            enc_weights,
            enc_gain,
            False,
            seqs_here,
            length,
        )
        grads_in.append(grad_start.reshape(seqs_here, length, wide_dim))
        batch_weights = enc_wgrads + dec_wgrads
        batch_small = enc_small + dec_small
        if batch_index == 0:
            weight_sums = batch_weights
            small_sums = batch_small
        else:
            weight_sums = jax.tree.map(jnp.add, weight_sums, batch_weights)
            small_sums = jax.tree.map(jnp.add, small_sums, batch_small)
    in_shards = (
        lax.psum_scatter(weight_sums[0], ("dp", "seq"), scatter_dimension=0, tiled=True),
        lax.psum_scatter(weight_sums[3], ("dp", "seq"), scatter_dimension=0, tiled=True),
    )
    conv_shards = (
        lax.psum_scatter(weight_sums[1], ("dp", "seq"), scatter_dimension=0, tiled=True),
        lax.psum_scatter(weight_sums[4], ("dp", "seq"), scatter_dimension=0, tiled=True),
    )
    out_shards = (
        lax.psum_scatter(weight_sums[2], ("dp", "seq"), scatter_dimension=0, tiled=True),
        lax.psum_scatter(weight_sums[5], ("dp", "seq"), scatter_dimension=0, tiled=True),
    )
    small_total = lax.psum(
        (small_sums[0], small_sums[1], small_sums[2], small_sums[3], small_sums[4], small_sums[5]),
        ("dp", "seq"),
    )
    output = jnp.stack(outputs)
    token_grad = jnp.stack(grads_in)
    return (
        output,
        token_grad,
        in_shards[0],
        conv_shards[0],
        out_shards[0],
        small_total[0],
        small_total[1],
        small_total[2],
        in_shards[1],
        conv_shards[1],
        out_shards[1],
        small_total[3],
        small_total[4],
        small_total[5],
    )


def solution(mesh):
    placed = (
        P(None, "dp", "seq", None),
        P(None, "dp", "seq"),
        P(None, "dp", "seq", None),
        P(("dp", "seq")),
        P(("dp", "seq")),
        P(("dp", "seq")),
        P(),
        P(),
        P(),
        P(("dp", "seq")),
        P(("dp", "seq")),
        P(("dp", "seq")),
        P(),
        P(),
        P(),
    )
    return jax.shard_map(
        per_device,
        mesh=mesh,
        in_specs=placed,
        out_specs=(
            P(None, "dp", "seq", None),
            P(None, "dp", "seq", None),
            P(("dp", "seq")),
            P(("dp", "seq")),
            P(("dp", "seq")),
            P(),
            P(),
            P(),
            P(("dp", "seq")),
            P(("dp", "seq")),
            P(("dp", "seq")),
            P(),
            P(),
            P(),
        ),
        check_vma=False,
    )
```

profile of v0, /device:TPU:0, one launch (start us, length us, event | category | flops | bytes accessed | tf_op | source)
XLA Modules:
  0.0 1316.4 jit_solution(9445602224511149685)
XLA Ops:
  48.7 314.7 %all-reduce.20.cloned.1.call-done = (bf16[1280000]{0:T(1024)(128)(2,1)}, bf16[3200000]{0:T(1024)(128)(2,1)}, bf16[1280000]{0:T(1024)(128)(2,1)}, bf16[1280000]{0...) async-done(((bf16[1280000]{0:T(1024)(128)(2,1)}, bf16[3200000]{0:T(1024)(128)(2,1)}, bf16[1280000]{0:T(1024)(128)(2,1)}, ...) | async-done | bytes 20480016
  363.4 6.9 reshape.508
  381.5 5.5 reshape.512
  394.1 6.9 reshape.513
  401.0 15.2 %reshape.511 = bf16[4000,800]{1,0:T(8,128)(2,1)} reshape(bf16[3200000]{0:T(1024)(128)(2,1)} %get-tuple-element.101) | data formatting | bytes 12800000 | tf_op jit(solution)/shard_map/reshape | solution.py:82
  417.4 6.8 fusion.224
  443.2 9.5 reshape.516
  452.7 9.5 reshape_reshape.8
  462.2 15.0 %reshape_reshape.9 = bf16[5,800,800]{2,1,0:T(8,128)(2,1)} reshape(bf16[3200000]{0:T(1024)(128)(2,1)} %get-tuple-element.101) | data formatting | bytes 12800000 | tf_op jit(solution)/shard_map/reshape;reshape | solution.py:208
  477.2 5.5 reshape.517
  513.6 7.2 add.497
  520.7 9.5 copy.36
  530.2 11.2 add.495
  586.8 6.7 convolution_add_fusion
  596.9 7.2 add.488
  604.1 6.8 copy.35
  611.0 8.0 add.493
  619.0 15.4 %copy.34 = f32[4000,800]{1,0:T(8,128)} copy(f32[4000,800]{0,1:T(8,128)} %convolution_add_fusion) | data formatting | bytes 25600000 | tf_op jit(solution)/shard_map/add | solution.py:305
  634.4 17.6 %add.486 = f32[3200000]{0:T(1024)} reshape(f32[4000,800]{1,0:T(8,128)} %copy.34) | data formatting | bytes 25600000 | tf_op jit(solution)/shard_map/add | solution.py:305
  665.9 5.6 multiply_reduce_fusion.15
  677.3 6.8 copy.33
  684.2 8.2 add.484
  708.4 44.4 %all-reduce.12 = (f32[3200]{0:T(1024)}, f32[3200]{0:T(1024)}, f32[1600]{0:T(1024)}, f32[3200]{0:T(1024)}, f32[3200]{0:T(1024)}, /*index=5*/f32[1600]{0:T(1024)}) all-reduce(f32[3200]{0:T(1024)S(1)} %add.489, f32[3200]{0:T(1024)S(1)} %add.490, f32[1600]{0:T(1024)S(1)} %add.491, ...), channel_id=1, replica_groups=mesh['dp'=8,'seq'=4] {'dp','seq'}, use_global_device_ids=true, to_apply=%region_57.58 | all-reduce | flops 16000 | bytes 128000 | tf_op jit(solution)/shard_map/psum | solution.py:319
  758.7 540.0 %all-reduce.18.cloned.1.call-done = (f32[1280000]{0:T(1024)}, f32[3200000]{0:T(1024)}, f32[1280000]{0:T(1024)}, f32[1280000]{0:T(1024)}, f32[1920000]{0:T(1024)}, /*index=5*/f32[1280000]{0:T(1024)}) async-done(((f32[1280000]{0:T(1024)}, f32[3200000]{0:T(1024)}, f32[1280000]{0:T(1024)}, f32[1280000]{0:T(1024)}, f32[1920000]{0:T(1024)}, /*index=5*/f32[1280000]{0:T(1024)}), (f32[1280000]{0:T(1024)}, ...) | async-done | bytes 40960016
  (522 shorter events, 209.4 us)
Async XLA Ops:
  7.2 356.2 %all-reduce.20.cloned.1.call-start = ((), (), s32[]{:S(2)}) async-start(), calls=%async_computation.1 | async-start | bytes 40960000
  31.1 1267.5 %all-reduce.18.cloned.1.call-start = ((), (), s32[]{:S(2)}) async-start(), calls=%async_computation | async-start | bytes 81920000
  31.8 13.2 %collective-permute-start.5 = (s32[1,16]{1,0:T(1,128)S(1)}, s32[1,16]{1,0:T(1,128)S(1)}, u32[]{:S(2)}, u32[]{:S(2)}) collective-permute-start(s32[1,16]{1,0:T(1,128)S(1)} %get-tuple-element.158), channel_id=1, source_target_pairs={{0,1},{1,2},{2,3},{4,5},{5,6},{6,7},{8,9},{9,10},{10,11},{12,13},{... | collective-permute-start | bytes 200 | tf_op jit(solution)/shard_map/ppermute | solution.py:30
  36.8 8.3 collective-permute-start.7
  38.1 7.6 collective-permute-start
  42.7 5.4 collective-permute-start.2
  45.0 465.1 %copy-start.40 = (f32[800]{0:T(1024)}, f32[800]{0:T(1024)S(1)}, u32[]{:S(2)}) copy-start(f32[800]{0:T(1024)S(1)} %get-tuple-element.134) | copy-start | bytes 9604
  45.0 465.1 %copy-start.43 = (f32[800]{0:T(1024)}, f32[800]{0:T(1024)S(1)}, u32[]{:S(2)}) copy-start(f32[800]{0:T(1024)S(1)} %get-tuple-element.195) | copy-start | bytes 9604
  45.7 370.5 %copy-start.89 = (pred[256]{0:T(512)(128)(4,1)}, pred[256]{0:T(512)(128)(4,1)S(1)}, u32[]{:S(2)}) copy-start(pred[256]{0:T(512)(128)(4,1)S(1)} %get-tuple-element.85) | copy-start | bytes 772
  45.7 371.4 %copy-start.92 = (pred[256]{0:T(512)(128)(4,1)}, pred[256]{0:T(512)(128)(4,1)S(1)}, u32[]{:S(2)}) copy-start(pred[256]{0:T(512)(128)(4,1)S(1)} %get-tuple-element.74) | copy-start | bytes 772
  48.7 375.5 %copy-start.95 = (pred[256]{0:T(512)(128)(4,1)}, pred[256]{0:T(512)(128)(4,1)S(1)}, u32[]{:S(2)}) copy-start(pred[256]{0:T(512)(128)(4,1)S(1)} %get-tuple-element.82) | copy-start | bytes 772
  48.7 376.3 %copy-start.98 = (pred[256]{0:T(512)(128)(4,1)}, pred[256]{0:T(512)(128)(4,1)S(1)}, u32[]{:S(2)}) copy-start(pred[256]{0:T(512)(128)(4,1)S(1)} %get-tuple-element.71) | copy-start | bytes 772
  377.9 38.3 %collective-permute-start.6 = (bf16[1,8,800]{1,2,0:T(8,128)(2,1)}, bf16[1,8,800]{1,2,0:T(8,128)(2,1)S(1)}, u32[]{:S(2)}, u32[]{:S(2)}) collective-permute-start(bf16[1,8,800]{1,2,0:T(8,128)(2,1)} %get-tuple-element.133), channel_id=1, source_target_pairs={{0,1},{1,2},{2,3},{4,5},{5,6},{6,7},{8,9},{9,10},{10,11},{12,13},{... | collective-permute-start | bytes 38408 | tf_op jit(solution)/shard_map/ppermute | solution.py:30
  387.0 37.8 %collective-permute-start.3 = (bf16[1,8,800]{1,2,0:T(8,128)(2,1)S(1)}, bf16[1,8,800]{1,2,0:T(8,128)(2,1)S(1)}, u32[]{:S(2)}, u32[]{:S(2)}) collective-permute-start(bf16[1,8,800]{1,2,0:T(8,128)(2,1)S(1)} %get-tuple-element.130), channel_id=1, source_target_pairs={{1,0},{2,1},{3,2},{5,4},{6,5},{7,6},{9,8},{10,9},{11,10},{13,12},{... | collective-permute-start | bytes 38408 | tf_op jit(solution)/shard_map/ppermute | solution.py:31
  388.3 36.0 %collective-permute-start.1 = (bf16[1,8,800]{1,2,0:T(8,128)(2,1)}, bf16[1,8,800]{1,2,0:T(8,128)(2,1)S(1)}, u32[]{:S(2)}, u32[]{:S(2)}) collective-permute-start(bf16[1,8,800]{1,2,0:T(8,128)(2,1)} %get-tuple-element.131), channel_id=1, source_target_pairs={{0,1},{1,2},{2,3},{4,5},{5,6},{6,7},{8,9},{9,10},{10,11},{12,13},{... | collective-permute-start | bytes 38408 | tf_op jit(solution)/shard_map/ppermute | solution.py:30
  392.8 23.9 %collective-permute-start.8 = (bf16[1,8,800]{1,2,0:T(8,128)(2,1)}, bf16[1,8,800]{1,2,0:T(8,128)(2,1)S(1)}, u32[]{:S(2)}, u32[]{:S(2)}) collective-permute-start(bf16[1,8,800]{1,2,0:T(8,128)(2,1)} %get-tuple-element.132), channel_id=1, source_target_pairs={{1,0},{2,1},{3,2},{5,4},{6,5},{7,6},{9,8},{10,9},{11,10},{13,12},{... | collective-permute-start | bytes 38408 | tf_op jit(solution)/shard_map/ppermute | solution.py:31
  438.6 47.8 %collective-permute-start.4 = (bf16[1,16,800]{1,2,0:T(8,128)(2,1)S(1)}, bf16[1,16,800]{1,2,0:T(8,128)(2,1)S(1)}, u32[]{:S(2)}, u32[]{:S(2)}) collective-permute-start(bf16[1,16,800]{1,2,0:T(8,128)(2,1)S(1)} %slice.360), channel_id=1, source_target_pairs={{0,1},{1,2},{2,3},{4,5},{5,6},{6,7},{8,9},{9,10},{10,11},{12,13},{... | collective-permute-start | bytes 76808 | tf_op jit(solution)/shard_map/ppermute | solution.py:20
  482.9 8.3 collective-permute-start.9
  503.0 38.5 %collective-permute-start.10 = (bf16[1,16,800]{1,2,0:T(8,128)(2,1)S(1)}, bf16[1,16,800]{1,2,0:T(8,128)(2,1)S(1)}, u32[]{:S(2)}, u32[]{:S(2)}) collective-permute-start(bf16[1,16,800]{1,2,0:T(8,128)(2,1)S(1)} %slice.382), channel_id=1, source_target_pairs={{1,0},{2,1},{3,2},{5,4},{6,5},{7,6},{9,8},{10,9},{11,10},{13,12},{... | collective-permute-start | bytes 76808 | tf_op jit(solution)/shard_map/ppermute | solution.py:20
  504.3 44.0 %collective-permute-start.13 = (bf16[1,16,800]{1,2,0:T(8,128)(2,1)}, bf16[1,16,800]{1,2,0:T(8,128)(2,1)S(1)}, u32[]{:S(2)}, u32[]{:S(2)}) collective-permute-start(bf16[1,16,800]{1,2,0:T(8,128)(2,1)} %slice.391), channel_id=1, source_target_pairs={{1,0},{2,1},{3,2},{5,4},{6,5},{7,6},{9,8},{10,9},{11,10},{13,12},{... | collective-permute-start | bytes 76808 | tf_op jit(solution)/shard_map/ppermute | solution.py:20
  567.4 97.3 %collective-permute-start.15 = (bf16[1,8,800]{1,2,0:T(8,128)(2,1)}, bf16[1,8,800]{1,2,0:T(8,128)(2,1)S(1)}, u32[]{:S(2)}, u32[]{:S(2)}) collective-permute-start(bf16[1,8,800]{1,2,0:T(8,128)(2,1)} %get-tuple-element.128), channel_id=1, source_target_pairs={{0,1},{1,2},{2,3},{4,5},{5,6},{6,7},{8,9},{9,10},{10,11},{12,13},{... | collective-permute-start | bytes 38408 | tf_op jit(solution)/shard_map/ppermute | solution.py:30
  572.6 89.7 %collective-permute-start.14 = (bf16[1,8,800]{1,2,0:T(8,128)(2,1)}, bf16[1,8,800]{1,2,0:T(8,128)(2,1)}, u32[]{:S(2)}, u32[]{:S(2)}) collective-permute-start(bf16[1,8,800]{1,2,0:T(8,128)(2,1)} %get-tuple-element.129), channel_id=1, source_target_pairs={{1,0},{2,1},{3,2},{5,4},{6,5},{7,6},{9,8},{10,9},{11,10},{13,12},{... | collective-permute-start | bytes 38408 | tf_op jit(solution)/shard_map/ppermute | solution.py:31
  576.7 77.8 %collective-permute-start.12 = (bf16[1,8,800]{1,2,0:T(8,128)(2,1)}, bf16[1,8,800]{1,2,0:T(8,128)(2,1)}, u32[]{:S(2)}, u32[]{:S(2)}) collective-permute-start(bf16[1,8,800]{1,2,0:T(8,128)(2,1)} %get-tuple-element.126), channel_id=1, source_target_pairs={{0,1},{1,2},{2,3},{4,5},{5,6},{6,7},{8,9},{9,10},{10,11},{12,13},{... | collective-permute-start | bytes 38408 | tf_op jit(solution)/shard_map/ppermute | solution.py:30
  581.9 70.1 %collective-permute-start.11 = (bf16[1,8,800]{1,2,0:T(8,128)(2,1)}, bf16[1,8,800]{1,2,0:T(8,128)(2,1)}, u32[]{:S(2)}, u32[]{:S(2)}) collective-permute-start(bf16[1,8,800]{1,2,0:T(8,128)(2,1)} %get-tuple-element.127), channel_id=1, source_target_pairs={{1,0},{2,1},{3,2},{5,4},{6,5},{7,6},{9,8},{10,9},{11,10},{13,12},{... | collective-permute-start | bytes 38408 | tf_op jit(solution)/shard_map/ppermute | solution.py:31
  (146 other events, 3328.6 us)
Sparse Core Ops, SparseCore 0:
  31.2 332.1 all-reduce.19
  692.6 605.9 all-reduce.17
where the time goes:
time: 1330 us; the launch traced here: 1320 us
  waiting for transfers between devices  857 us (64%)
  local copies, waits for them, and re-layouts  219 us (16%)
  matrix products  105 us (8%)
  starting transfers between devices  45.7 us (3%)
  blocking collectives  44.4 us (3%)
  other arithmetic  28.2 us (2%)
  between operations  17 us (1%)
    unnamed x4, waiting for transfers between devices  855 us
    add x10, local copies, waits for them, and re-layouts, per_device(): weight_sums = jax.tree.map(jnp.add, weight_sums, batch_weights)  98 us
    psum x1, blocking collectives, per_device(): lax.psum((small_sums[0], small_sums[1], small_sums[2], small_sums[3], sma...  44.4 us
    unnamed x326, local copies, waits for them, and re-layouts  42.1 us
    ppermute x6, starting transfers between devices, extended(): before = lax.ppermute(last, axis, up)  27.2 us
  transfers between devices with their start and end apart: 18, of which 3 were waited for; matrix products, arithmetic and copies ran while one was open for 17% of the time, Pallas kernels for 0%

commit v1 on v0

--- a/solution.py
+++ b/solution.py
@@ -1,8 +1,13 @@
+import functools
+
 import jax
 import jax.numpy as jnp
 from jax import lax
+from jax.experimental import pallas as pl
+from jax.experimental.pallas import tpu as pltpu
 from jax.sharding import PartitionSpec as P
 
+MESH = pl.DeviceIdType.MESH
 D2 = 1600
 D = 800
 ENCODER_TAPS = 5
@@ -74,34 +79,6 @@
         )
         pieces.append(jnp.where(same_doc[:, :, None], shifted, jnp.zeros_like(shifted)))
     return jnp.concatenate(pieces, axis=-1)
-
-
-def shape_weights(flat_three):
-    return (
-        flat_three[0].reshape(D2, D),
-        flat_three[1].reshape(-1, D),
-        flat_three[2].reshape(D, D2),
-    )
-
-
-def fetch_forward(input_weight, convolution_weight, output_weight):
-    return shape_weights(
-        (
-            lax.all_gather(input_weight, ("dp", "seq"), axis=0, tiled=True),
-            lax.all_gather(convolution_weight, ("dp", "seq"), axis=0, tiled=True),
-            lax.all_gather(output_weight, ("dp", "seq"), axis=0, tiled=True),
-        )
-    )
-
-
-def fetch_backward(input_weight, convolution_weight, output_weight):
-    return shape_weights(
-        (
-            lax.all_gather(input_weight, ("dp", "seq"), axis=0, tiled=True),
-            lax.all_gather(convolution_weight, ("dp", "seq"), axis=0, tiled=True),
-            lax.all_gather(output_weight, ("dp", "seq"), axis=0, tiled=True),
-        )
-    )
 
 
 def block_forward(
@@ -200,13 +177,15 @@
         lead_rows = reach_rows
     back_stack = stacked_taps(
         padded, lead_rows, seg_pad, segment_leading, [-offset for offset in shift_offsets], length
-    )
-    back_stack = back_stack.reshape(-1, len(shift_offsets), narrow)
-    grad_act = jnp.einsum(
-        "nkj,kij->ni",
-        back_stack,
-        convolution_weight.reshape(len(shift_offsets), narrow, narrow),
-        preferred_element_type=jnp.float32,
+    ).reshape(seqs_here * length, -1)
+    grad_act = sum(
+        lax.dot_general(
+            back_stack[:, k * narrow : (k + 1) * narrow],
+            convolution_weight[k * narrow : (k + 1) * narrow],
+            (((1,), (1,)), ((), ())),
+            preferred_element_type=jnp.float32,
+        )
+        for k in range(len(shift_offsets))
     )
     grad_act = grad_act * silu_slope(hidden_two)
     grad_narrow, gain_two, shift_two = norm_back(
@@ -228,115 +207,741 @@
     grad_shift = jnp.concatenate([shift_one, shift_two, shift_three])
     return (
         grad_input,
-        (grad_w_in.reshape(-1), grad_w_conv.reshape(-1), grad_w_out.reshape(-1)),
+        (grad_w_in, grad_w_conv, grad_w_out),
         (grad_gain, grad_shift, grad_bias),
     )
 
 
+F32, BF = jnp.float32, jnp.bfloat16
+T16 = 16
+MATS = ((50, 800, False), (125, 800, True), (25, 1600, False), (50, 800, False), (75, 800, True), (25, 1600, False))
+
+def tile_at(n, s): return (n * s + T16 - 1) // T16
+
+def places():
+    dp = lax.axis_index("dp"); z = lax.axis_index("seq")
+    return dp // 4, (dp // 2) % 2, dp % 2, z
+
+def dev(y, x, c, z): return ((y * 2 + x) * 2 + c, z)
+def shard(y, x, c, z): return ((y * 2 + x) * 2 + c) * 4 + z
+
+def when(cond, f):
+    if cond is None: f()
+    else: pl.when(cond)(f)
+
+def both(a, b):
+    if a is None: return b
+    if b is None: return a
+    return jnp.logical_and(a, b)
+
+def greet(y, x, c, z):
+    barrier = pltpu.get_barrier_semaphore()
+    dp = (y * 2 + x) * 2 + c
+    far_next = jnp.logical_and(z == 3, dp < 7)
+    far_prev = jnp.logical_and(z == 0, dp > 0)
+    peers = [(dev(y, 1 - x, c, z), None), (dev(1 - y, x, c, z), None), (dev(y, x, 1 - c, z), None)]
+    peers += [((dp, (z + i) % 4), None) for i in (1, 2, 3)]
+    peers += [((jnp.minimum(dp + 1, 7), 0), far_next), ((jnp.maximum(dp - 1, 0), 3), far_prev)]
+    for d, cond in peers:
+        when(cond, lambda d=d: pl.semaphore_signal(barrier, inc=1, device_id=d, device_id_type=MESH))
+    pl.semaphore_wait(barrier, 6 + jnp.where(far_next, 1, 0) + jnp.where(far_prev, 1, 0))
+
+class Sender:
+    def __init__(self, sem): self.sem, self.sent = sem, []
+    def __call__(self, src, dst, rsem, target, cond=None):
+        d = pltpu.make_async_remote_copy(src_ref=src, dst_ref=dst, send_sem=self.sem.at[self.k], recv_sem=rsem,
+                                         device_id=target, device_id_type=MESH)
+        self.sent.append((d, cond))
+        when(cond, d.start)
+    def next(self): self.k = getattr(self, "k", -1) + 1
+    def finish(self):
+        for d, cond in self.sent: when(cond, d.wait_send)
+
+def arrive(dst, rsem, ssem, me):
+    pltpu.make_async_remote_copy(src_ref=dst, dst_ref=dst, send_sem=ssem, recv_sem=rsem, device_id=me, device_id_type=MESH).wait_recv()
+
+def sizes(n, s, units):
+    f, exact = (n * units) // T16, (n * units) % T16 == 0
+    if exact: return [(f, None)]
+    cnt = tile_at(n, s + units) - tile_at(n, s)
+    return [(f, cnt == f), (f + 1, cnt == f + 1)]
+
+def rows_at(n, s, tiles): return pl.ds(pl.multiple_of(tile_at(n, s) * T16, T16), tiles * T16)
+
+def gather_kernel(order, *refs):
+    nm = len(MATS)
+    inp, out = refs[:nm], refs[nm:2 * nm]
+    own, nxt = refs[2 * nm:3 * nm], refs[3 * nm:4 * nm]
+    ext, exw, send_sem, recv_sem, n_sem, local_sem = refs[4 * nm:]
+    y, x, c, z = places()
+    X, Y, C = 1 - x, 1 - y, 1 - c
+    dp = (y * 2 + x) * 2 + c
+    me = shard(y, x, c, z)
+    greet(y, x, c, z)
+    here = dev(y, x, C, z)
+    snd = Sender(send_sem)
+    has_up, has_down = z < 3, z > 0
+    tX, tY, tC = dev(y, X, c, z), dev(Y, x, c, z), dev(y, x, C, z)
+    tU, tD = dev(y, x, c, jnp.minimum(z + 1, 3)), dev(y, x, c, jnp.maximum(z - 1, 0))
+    has_prev, has_next = me > 0, me < 31
+    prev = jnp.maximum(me - 1, 0)
+    tP = (prev // 4, prev % 4)
+    for m, (n, L, _) in enumerate(MATS):
+        snd.next()
+        snd(inp[m].at[pl.ds(0, T16)], nxt[m], n_sem.at[m], tP, has_prev)
+    def build(m):
+        n, L, _ = MATS[m]
+        e = exw if L == 1600 else ext
+        tiles = n // T16 + 1
+        pl.when(has_next)(lambda: arrive(nxt[m], n_sem.at[m], send_sem.at[0], here))
+        e[0:n, :] = inp[m][...].astype(F32)
+        e[n:n + T16, :] = nxt[m][...].astype(F32)
+        o = tile_at(n, me) * T16 - n * me
+        size = -(-max(n + T16, 15 + tiles * T16) // 8) * 8
+        v = pltpu.roll(e[0:size, :], lax.rem(size - o, size), axis=0)
+        own[m][...] = v[0:tiles * T16].astype(BF)
+    locals_ = []
+    def send(m, s, target, cond=None, mine=False):
+        n = MATS[m][0]
+        snd.next()
+        for tiles, c2 in sizes(n, s, 1):
+            r = rows_at(n, s, tiles)
+            src = own[m].at[pl.ds(0, tiles * T16)] if mine else out[m].at[r]
+            snd(src, out[m].at[r], recv_sem.at[s, m], target, both(cond, c2))
+    def wait(m, s, cond=None):
+        n = MATS[m][0]
+        for tiles, c2 in sizes(n, s, 1):
+            when(both(cond, c2), lambda: arrive(out[m].at[rows_at(n, s, tiles)], recv_sem.at[s, m], send_sem.at[0], here))
+    def first(m): return tX if MATS[m][2] else tY
+    def second(m): return tY if MATS[m][2] else tX
+    def st_own(m):
+        build(m)
+        send(m, me, first(m), None, True)
+        send(m, me, tU, has_up, True)
+        send(m, me, tD, has_down, True)
+        send(m, me, second(m), None, True)
+        send(m, me, tC, None, True)
+        for tiles, c2 in sizes(MATS[m][0], me, 1):
+            l = pltpu.make_async_copy(own[m].at[pl.ds(0, tiles * T16)], out[m].at[rows_at(MATS[m][0], me, tiles)], local_sem.at[m])
+            locals_.append((l, c2)); when(c2, l.start)
+    def st_z(m, d):
+        for o, has, t, has_t in ((z - d, z - d >= 0, tU, has_up), (z + d, z + d <= 3, tD, has_down)):
+            s = shard(y, x, c, jnp.clip(o, 0, 3))
+            wait(m, s, has)
+            send(m, s, first(m), has)
+            if d < 3: send(m, s, t, jnp.logical_and(has, has_t))
+            send(m, s, second(m), has)
+            send(m, s, tC, has)
+    def zorder(j):
+        if j == 0: return [(z, None)]
+        return [(jnp.clip(z - j, 0, 3), z - j >= 0), (jnp.clip(z + j, 0, 3), z + j <= 3)]
+    def st_f(m, j):
+        yy, xx = (y, X) if MATS[m][2] else (Y, x)
+        for o, cond in zorder(j):
+            s = shard(yy, xx, c, o)
+            wait(m, s, cond)
+            send(m, s, second(m), cond)
+            send(m, s, tC, cond)
+    def st_s(m, j):
+        yy, xx = (Y, x) if MATS[m][2] else (y, X)
+        for o, cond in zorder(j):
+            s = shard(yy, xx, c, o)
+            wait(m, s, cond)
+            send(m, s, tC, cond)
+    def st_d(m, j):
+        for o, cond in zorder(j):
+            s = shard(Y, X, c, o)
+            wait(m, s, cond)
+            send(m, s, tC, cond)
+    ev = []
+    for m in range(nm):
+        def add(t, f, *a): ev.append((order(m, t), m, functools.partial(f, m, *a)))
+        add(0, st_own)
+        for d in (1, 2, 3): add(d, st_z, d)
+        for j in range(4):
+            add(1.1 + j, st_f, j)
+            add(1.2 + j, st_s, j)
+            add(2.3 + j, st_d, j)
+    for _, _, f in sorted(ev, key=lambda e: (e[0], e[1])): f()
+    for m in range(nm):
+        for q in range(16): wait(m, shard(q // 8, (q // 4) % 2, C, q % 4))
+    snd.finish()
+    for l, c2 in locals_: when(c2, l.wait)
+
+def gather(shards, order, cid=0):
+    nm = len(MATS)
+    any_ = pl.BlockSpec(memory_space=pl.ANY)
+    vm = pl.BlockSpec(memory_space=pltpu.VMEM)
+    V = pltpu.VMEM
+    D_ = pltpu.SemaphoreType.DMA
+    return pl.pallas_call(
+        functools.partial(gather_kernel, order),
+        out_shape=[jax.ShapeDtypeStruct((n * 32, L), BF) for n, L, _ in MATS],
+        in_specs=[vm] * nm, out_specs=[any_] * nm,
+        scratch_shapes=[V(((n // T16 + 1) * T16, L), BF) for n, L, _ in MATS] + [V((T16, L), BF) for n, L, _ in MATS]
+        + [V((144, 800), F32), V((48, 1600), F32), D_((nm * 64,)), D_((32, nm)), D_((nm,)), D_((nm,))],
+        compiler_params=pltpu.CompilerParams(collective_id=cid, has_side_effects=True, vmem_limit_bytes=24 * 2**20),
+    )(*shards)
+
+def scatter_kernel(order, *refs):
+    nm = len(MATS)
+    small_in, g = refs[0], refs[1:1 + nm]
+    small_out, out = refs[1 + nm], refs[2 + nm:2 + 2 * nm]
+    p = 2 + 2 * nm
+    own, rbc, rb1, rb2, rbz = (refs[p + i * nm:p + (i + 1) * nm] for i in range(5))
+    p += 5 * nm
+    tail, res = refs[p:p + nm], refs[p + nm:p + 2 * nm]
+    p += 2 * nm
+    (sm_a, sm_r, sm_z, send_sem, c_sem, s1_sem, s2_sem, z_sem, t_sem, local_sem, sm_sem) = refs[p:]
+    y, x, c, z = places()
+    X, Y, C = 1 - x, 1 - y, 1 - c
+    dp = (y * 2 + x) * 2 + c
+    me = shard(y, x, c, z)
+    greet(y, x, c, z)
+    snd = Sender(send_sem)
+    has_up, has_down = z < 3, z > 0
+    tX, tY, tC = dev(y, X, c, z), dev(Y, x, c, z), dev(y, x, C, z)
+    tU, tD = dev(y, x, c, jnp.minimum(z + 1, 3)), dev(y, x, c, jnp.maximum(z - 1, 0))
+    edge = jnp.logical_or(z == 0, z == 3)
+    mid = jnp.logical_not(edge)
+    def wait(dst, rsem): arrive(dst, rsem, send_sem.at[0], tC)
+    def groups(m):
+        if MATS[m][2]: return [(Y, X), (y, X), (Y, x), (y, x)]
+        return [(Y, X), (Y, x), (y, X), (y, x)]
+    def first_shard(yy, xx, cc): return ((yy * 2 + xx) * 2 + cc) * 4
+    def add(refs_, dst, r0, tiles):
+        def body(i, _):
+            r = pl.ds(pl.multiple_of(r0 + i * T16, T16), T16)
+            t = refs_[0][r, :].astype(F32)
+            for q in refs_[1:]: t = t + q[r, :].astype(F32)
+            dst(i, r, t)
+            return 0
+        lax.fori_loop(0, tiles, body, 0)
+    def st_start(m):
+        n = MATS[m][0]
+        for i, (yy, xx) in enumerate(groups(m)):
+            q = yy * 2 + xx
+            snd.next()
+            s = first_shard(yy, xx, C)
+            for tiles, c2 in sizes(n, s, 4):
+                snd(g[m].at[rows_at(n, s, tiles)], rbc[m].at[q, pl.ds(0, tiles * T16)], c_sem.at[i, m], tC, c2)
+            s = first_shard(yy, xx, c)
+            for tiles, c2 in sizes(n, s, 4):
+                when(c2, pltpu.make_async_copy(g[m].at[rows_at(n, s, tiles)], own[m].at[q, pl.ds(0, tiles * T16)], local_sem.at[i, m]).start)
+    def got(m, i):
+        n = MATS[m][0]
+        yy, xx = groups(m)[i]
+        q = yy * 2 + xx
+        s = first_shard(yy, xx, c)
+        for tiles, c2 in sizes(n, s, 4):
+            r = pl.ds(0, tiles * T16)
+            def f():
+                wait(rbc[m].at[q, r], c_sem.at[i, m])
+                pltpu.make_async_copy(rbc[m].at[q, r], own[m].at[q, r], local_sem.at[i, m]).wait()
+            when(c2, f)
+        return q, s, tile_at(n, s + 4) - tile_at(n, s)
+    def st_1(m, i):
+        n, _, xf = MATS[m]
+        q, s, tiles = got(m, i)
+        rest = (Y, y)[i] if xf else (X, x)[i]
+        ow = own[m].at[q]
+        def put(i, r, t): ow[r, :] = t.astype(BF)
+        add([ow, rbc[m].at[q]], put, 0, tiles)
+        snd.next()
+        for t, c2 in sizes(n, s, 4):
+            snd(own[m].at[q, pl.ds(0, t * T16)], rb1[m].at[rest, pl.ds(0, t * T16)], s1_sem.at[i, m], tX if xf else tY, c2)
+    def wait1(m, s, slot, i):
+        for t, c2 in sizes(MATS[m][0], s, 4):
+            when(c2, lambda: wait(rb1[m].at[slot, pl.ds(0, t * T16)], s1_sem.at[i, m]))
+    def st_2(m):
+        n, _, xf = MATS[m]
+        q, s, tiles = got(m, 2)
+        rest = Y if xf else X
+        wait1(m, s, rest, 0)
+        ow = own[m].at[q]
+        def put(i, r, t): ow[r, :] = t.astype(BF)
+        add([ow, rbc[m].at[q], rb1[m].at[rest]], put, 0, tiles)
+        snd.next()
+        for t, c2 in sizes(n, s, 4):
+            snd(own[m].at[q, pl.ds(0, t * T16)], rb2[m].at[pl.ds(0, t * T16)], s2_sem.at[m], tY if xf else tX, c2)
+    def st_3(m):
+        n, _, xf = MATS[m]
+        q, s, tiles = got(m, 3)
+        wait1(m, s, y if xf else x, 1)
+        for t, c2 in sizes(n, s, 4):
+            when(c2, lambda: wait(rb2[m].at[pl.ds(0, t * T16)], s2_sem.at[m]))
+    def column(m, zz):
+        n, _, xf = MATS[m]
+        q = y * 2 + x
+        s0 = first_shard(y, x, c)
+        r0 = (tile_at(n, s0 + zz) - tile_at(n, s0)) * T16
+        return [own[m].at[q], rbc[m].at[q], rb1[m].at[y if xf else x], rb2[m]], r0, tile_at(n, s0 + zz + 1) - tile_at(n, s0 + zz), s0 + zz
+    def zwait(m, d, s, r0):
+        for t, c2 in sizes(MATS[m][0], s, 1):
+            when(c2, lambda: wait(rbz[m].at[d, pl.ds(pl.multiple_of(r0, T16), t * T16)], z_sem.at[d, s % 4, m]))
+    def zsend(m, zz, d, comes, cond):
+        refs_, r0, tiles, s = column(m, zz)
+        ow = refs_[0]
+        def put(i, r, t): ow[r, :] = t.astype(BF)
+        @pl.when(cond)
+        def _():
+            more = []
+            if comes:
+                zwait(m, d, s, r0)
+                more = [rbz[m].at[d]]
+            add(refs_ + more, put, r0, tiles)
+        t = tuple(jnp.where(d == 0, a, b) for a, b in zip(tU, tD))
+        snd.next()
+        for k, c2 in sizes(MATS[m][0], s, 1):
+            r = pl.ds(pl.multiple_of(r0, T16), k * T16)
+            snd(ow.at[r], rbz[m].at[d, r], z_sem.at[d, zz, m], t, both(cond, c2))
+    def st_z1(m):
+        d = jnp.where(z == 0, 0, 1)
+        for i in range(3): zsend(m, jnp.where(z == 0, 3 - i, i), d, False, edge)
+    def st_z2(m):
+        d = jnp.where(z == 1, 0, 1)
+        for i in range(2): zsend(m, jnp.where(z == 1, 3 - i, i), d, True, mid)
+    def st_z3(m):
+        d = jnp.where(z == 1, 1, 0)
+        zsend(m, jnp.where(z == 1, 0, 3), d, True, mid)
+    nxt = jnp.minimum(me + 1, 31)
+    tN = (nxt // 4, nxt % 4)
+    def st_z4(m):
+        n = MATS[m][0]
+        refs_, r0, tiles, s = column(m, z)
+        d = jnp.where(z == 0, 1, 0)
+        zwait(m, d, s, r0)
+        def put(i, r, t): res[m][pl.ds(pl.multiple_of((i + 1) * T16, T16), T16), :] = t
+        @pl.when(edge)
+        def _(): add(refs_ + [rbz[m].at[d]], put, r0, tiles)
+        @pl.when(mid)
+        def _():
+            zwait(m, 1, s, r0)
+            add(refs_ + [rbz[m].at[0], rbz[m].at[1]], put, r0, tiles)
+        snd.next()
+        snd(res[m].at[pl.ds(pl.multiple_of(tiles * T16, T16), T16)], tail[m], t_sem.at[m], tN, me < 31)
+    def st_out(m):
+        n, L, _ = MATS[m]
+        o = tile_at(n, me) * T16 - n * me
+        pl.when(me > 0)(lambda: wait(tail[m], t_sem.at[m]))
+        size = res[m].shape[0]
+        res[m][0:T16, :] = tail[m][...]
+        v = pltpu.roll(res[m][...], lax.rem(size - (T16 - o), size), axis=0)
+        out[m][...] = v[0:n]
+    def sm_pair(i, src, target, dst):
+        snd.next()
+        snd(src, sm_r.at[i], sm_sem.at[i], target)
+        wait(sm_r.at[i], sm_sem.at[i])
+        dst[...] = src[...] + sm_r[i]
+    def sm_0(): sm_pair(0, small_in, tC, sm_a.at[0])
+    def sm_1(): sm_pair(1, sm_a.at[0], tX, sm_a.at[1])
+    def sm_2():
+        sm_pair(2, sm_a.at[1], tY, sm_a.at[2])
+        for i in (1, 2, 3):
+            snd.next()
+            snd(sm_a.at[2], sm_z.at[z], sm_sem.at[3 + i - 1], (dp, (z + i) % 4))
+    def sm_3():
+        sm_z[z] = sm_a[2]
+        for i in (1, 2, 3): wait(sm_z.at[(z - i) % 4], sm_sem.at[3 + i - 1])
+        small_out[...] = ((sm_z[0] + sm_z[1]) + sm_z[2]) + sm_z[3]
+    ev = []
+    for k, m in enumerate((5, 4, 3, 2, 1, 0)):
+        def a(t, f, *ar): ev.append((order(k, t), k, functools.partial(f, m, *ar)))
+        a(0, st_start)
+        a(1, st_1, 0); a(1.3, st_1, 1); a(2, st_2); a(3, st_3); a(3.1, st_z1); a(4, st_z2); a(5, st_z3); a(6, st_z4)
+        ev.append((1000, k, functools.partial(st_out, m)))
+    ev += [(order(0, 0) , 10, sm_0), (order(1, 1), 10, sm_1), (order(2, 1), 10, sm_2), (order(5, 3), 10, sm_3)]
+    for _, _, f in sorted(ev, key=lambda e: (e[0], e[1])): f()
+    snd.finish()
+
+def scatter(small, grads, order, cid=1):
+    nm = len(MATS)
+    any_ = pl.BlockSpec(memory_space=pl.ANY)
+    vm = pl.BlockSpec(memory_space=pltpu.VMEM)
+    V = pltpu.VMEM
+    D_ = pltpu.SemaphoreType.DMA
+    gr = [(4 * n // T16 + 1) * T16 for n, _, _ in MATS]
+    def bufs(*lead): return [V(lead + (r, L), BF) for r, (_, L, _) in zip(gr, MATS)]
+    return pl.pallas_call(
+        functools.partial(scatter_kernel, order),
+        out_shape=[jax.ShapeDtypeStruct(small.shape, F32)] + [jax.ShapeDtypeStruct((n, L), F32) for n, L, _ in MATS],
+        in_specs=[vm] + [any_] * nm, out_specs=[vm] * (nm + 1),
+        scratch_shapes=bufs(4) + bufs(4) + bufs(2) + bufs() + bufs(2)
+        + [V((T16, L), F32) for _, L, _ in MATS] + [V((T16 + (n // T16 + 1) * T16, L), F32) for n, L, _ in MATS]
+        + [V((3,) + small.shape, F32), V((3,) + small.shape, F32), V((4,) + small.shape, F32),
+           D_((nm * 16 + 8,)), D_((4, nm)), D_((2, nm)), D_((nm,)), D_((2, 4, nm)), D_((nm,)), D_((4, nm)), D_((6,))],
+        compiler_params=pltpu.CompilerParams(collective_id=cid, has_side_effects=True, vmem_limit_bytes=56 * 2**20),
+    )(small, *grads)
+
+
+EPS = 1e-5
+W, N_ = 1600, 800
+ROWS, LEN_ = 512, 256
+
+def lane_tiles(n): return [(i, min(128, n - i)) for i in range(0, n, 128)]
+
+def norm_of(v):
+    c = v - jnp.mean(v, axis=-1, keepdims=True)
+    r = lax.rsqrt(jnp.mean(c * c, axis=-1, keepdims=True) + EPS)
+    return c * r, r
+
+def sigmoid(h): return 1.0 / (1.0 + jnp.exp(-h))
+
+def slope(h):
+    s = sigmoid(h)
+    return s * (1.0 + h * (1.0 - s))
+
+def row_loop(step, body):
+    def it(i, _):
+        body(pl.multiple_of(i * step, step))
+        return 0
+    lax.fori_loop(0, ROWS // step, it, 0)
+
+def put_transposed(dst, r, val, step):
+    for c0, cn in lane_tiles(val.shape[1]):
+        dst[c0:c0 + cn, pl.ds(r, step)] = jnp.transpose(val[:, c0:c0 + cn]).astype(BF)
+
+def chunks(n, step):
+    return n // step, n % step
+
+def mm(lhs, w, out, epilogue=None, step=256):
+    n = w.shape[1]
+    full, rest = chunks(n, step)
+    def one(c0, cn):
+        t = jnp.dot(lhs[...], w[:, pl.ds(c0, cn)], preferred_element_type=F32)
+        if epilogue is None: out[:, pl.ds(c0, cn)] = t
+        else: epilogue(t, c0, cn)
+    def it(i, _):
+        one(pl.multiple_of(i * step, step), step)
+        return 0
+    lax.fori_loop(0, full, it, 0)
+    if rest: one(full * step, rest)
+
+def mm_taps(lhs, w, out, taps, step=256):
+    full, rest = chunks(N_, step)
+    def one(c0, cn):
+        t = None
+        for k in range(taps):
+            d = jnp.dot(lhs[k], w[k * N_:(k + 1) * N_, pl.ds(c0, cn)], preferred_element_type=F32)
+            t = d if t is None else t + d
+        out[:, pl.ds(c0, cn)] = t
+    def it(i, _):
+        one(pl.multiple_of(i * step, step), step)
+        return 0
+    lax.fori_loop(0, full, it, 0)
+    if rest: one(full * step, rest)
+
+TT = (((1,), (1,)), ((), ()))
+
+def mm_t(lhs, w, out, step=256):
+    full, rest = chunks(w.shape[0], step)
+    def one(c0, cn):
+        out[:, pl.ds(c0, cn)] = lax.dot_general(lhs[...], w[pl.ds(c0, cn), :], TT, preferred_element_type=F32)
+    def it(i, _):
+        one(pl.multiple_of(i * step, step), step)
+        return 0
+    lax.fori_loop(0, full, it, 0)
+    if rest: one(full * step, rest)
+
+def mm_taps_t(lhs, w, out, taps, step=256):
+    full, rest = chunks(N_, step)
+    def one(c0, cn):
+        t = None
+        for k in range(taps):
+            start = k * N_ + c0
+            if not isinstance(c0, int): start = pl.multiple_of(start, 16)
+            d = lax.dot_general(lhs[k], w[pl.ds(start, cn), :], TT, preferred_element_type=F32)
+            t = d if t is None else t + d
+        out[:, pl.ds(c0, cn)] = t
+    def it(i, _):
+        one(pl.multiple_of(i * step, step), step)
+        return 0
+    lax.fori_loop(0, full, it, 0)
+    if rest: one(full * step, rest)
+
+def fold8(v):
+    return jnp.sum(v.reshape(v.shape[0] // 8, 8, v.shape[1]), axis=0)
+
+def comp_kernel(tok_h, cot_h, ids_ref, ge_ref, gd_ref,
+                wie_h, wce_h, woe_h, wid_h, wcd_h, wod_h,
+                out_h, tg_h, small_ref, gie_h, gce_h, goe_h, gid_h, gcd_h, god_h,
+                wie, wce, woe, wid, wcd, wod, tok, mid, ue, ve, ud, vd, a1b, a3b, a1te, a1td, a2te, a2td, a3te, a3td,
+                ape, apd, gpe, idp, lk, big, st8, st16, acc1, acc2, acc3, accb,
+                in_sem, h_send, h_recv, g_sem, o_sem):
+    dp = lax.axis_index("dp"); z = lax.axis_index("seq")
+    has_up, has_down = z < 3, z > 0
+    tU, tD = (dp, jnp.minimum(z + 1, 3)), (dp, jnp.maximum(z - 1, 0))
+    gpd, gub, obuf, cot = ape, a3b, a1b, tok
+    loads = [pltpu.make_async_copy(s, d, in_sem.at[i]) for i, (s, d) in enumerate(
+        [(tok_h, tok), (wie_h, wie), (wce_h, wce), (woe_h, woe), (wid_h, wid), (wcd_h, wcd), (wod_h, wod)])]
+    for l in loads: l.start()
+    barrier = pltpu.get_barrier_semaphore()
+    for d, cond in ((tU, has_up), (tD, has_down)):
+        @pl.when(cond)
+        def _(d=d): pl.semaphore_signal(barrier, inc=1, device_id=d, device_id_type=MESH)
+    pl.semaphore_wait(barrier, jnp.where(has_up, 1, 0) + jnp.where(has_down, 1, 0))
+
+    def halo(k, buf, lead, reach, up, fill):
+        if up:
+            src, dst, target, can, arrives = buf.at[:, pl.ds(lead + LEN_ - reach, reach)], buf.at[:, pl.ds(lead - reach, reach)], tU, has_up, has_down
+        else:
+            src, dst, target, can, arrives = buf.at[:, pl.ds(lead, reach)], buf.at[:, pl.ds(lead + LEN_, reach)], tD, has_down, has_up
+        d = pltpu.make_async_remote_copy(src_ref=src, dst_ref=dst, send_sem=h_send.at[k], recv_sem=h_recv.at[k], device_id=target, device_id_type=MESH)
+        pl.when(can)(d.start)
+        @pl.when(jnp.logical_not(arrives))
+        def _(): dst[...] = jnp.full(dst.shape, fill, buf.dtype)
+        return d, can, arrives
+    def halo_wait(h):
+        d, can, arrives = h
+        pl.when(arrives)(d.wait_recv)
+        pl.when(can)(d.wait_send)
+
+    idp[:, 16:16 + LEN_] = ids_ref[...]
+    h0, h1 = halo(0, idp, 16, 16, True, -1), halo(1, idp, 16, 16, False, -1)
+
+    OE = [4 * (k - 2) for k in range(5)]
+    OD = [8 * (k - 2) for k in range(3)]
+
+    def first_norm(x_of, par, a, at, load=None):
+        g, s = par[0:1, :], par[1:2, :]
+        def body(r):
+            n, _ = norm_of(x_of(r, 128))
+            h = n * g + s
+            a[pl.ds(r, 128), :] = (h * sigmoid(h)).astype(BF)
+        row_loop(128, body)
+        row_loop(128, lambda r: put_transposed(at, r, a[pl.ds(r, 128), :].astype(F32), 128))
+    def mid_norm(u, par, row, dst, at):
+        g, s = par[row:row + 1, 0:N_], par[row + 1:row + 2, 0:N_]
+        def body(r):
+            n, _ = norm_of(u[pl.ds(r, 128), :])
+            h = n * g + s
+            dst(r, 128, (h * sigmoid(h)).astype(BF))
+        row_loop(128, body)
+    def into(buf, lead):
+        def dst(r, n, v):
+            m = r // LEN_
+            buf[m, pl.ds(pl.multiple_of(r - m * LEN_ + lead, 8), n), :] = v.astype(buf.dtype)
+        return dst
+    def transpose_pad(buf, lead, at):
+        def it(i, _):
+            m, q = i // 2, i % 2
+            v = buf[m, pl.ds(pl.multiple_of(lead + q * 128, 8), 128), :]
+            put_transposed(at, pl.multiple_of(i * 128, 128), v, 128)
+            return 0
+        lax.fori_loop(0, 4, it, 0)
+    def stack(buf, lead, offsets):
+        def it(m, _):
+            rows = pl.ds(pl.multiple_of(m * LEN_, LEN_), LEN_)
+            own = idp[m, 16:16 + LEN_, :]
+            for k, o in enumerate(offsets):
+                same = idp[m, 16 + o:16 + o + LEN_, :] == own
+                for c0, cn in lane_tiles(N_):
+                    v = buf[m, lead + o:lead + o + LEN_, c0:c0 + cn]
+                    lk[k, rows, c0:c0 + cn] = jnp.where(same[:, :cn], v, 0.0).astype(BF)
+            return 0
+        lax.fori_loop(0, 2, it, 0)
+
+    def forward(x_of, par, a1t, a2t, a3t, wi, wc, wo, u, v, ap, lead, offsets, hal, base, finish):
+        first_norm(x_of, par, a1b, a1t)
+        loads[base].wait()
+        mm(a1b, wi, u)
+        mid_norm(u, par, 3, into(ap, lead), None)
+        hs = hal()
+        transpose_pad(ap, lead, a2t)
+        loads[base + 1].wait()
+        for h in hs: halo_wait(h)
+        stack(ap, lead, offsets)
+        mm_taps(lk, wc, v, len(offsets))
+        def keep3(r, n, val): a3b[pl.ds(r, n), :] = val
+        mid_norm(v, par, 5, keep3, None)
+        row_loop(128, lambda r: put_transposed(a3t, r, a3b[pl.ds(r, 128), :].astype(F32), 128))
+        loads[base + 2].wait()
+        bias = par[2:3, :]
+        mm(a3b, wo, None, epilogue=finish)
+
+    loads[0].wait()
+    tok_rows = lambda r, n: tok[pl.ds(r, n), :].astype(F32)
+    mid_rows = lambda r, n: mid[pl.ds(r, n), :]
+    def fin_e(t, c0, cn):
+        c = pl.ds(c0, cn)
+        mid[:, c] = tok[:, c].astype(F32) + (t + ge_ref[2:3, c])
+    halo_wait(h0); halo_wait(h1)
+    forward(tok_rows, ge_ref, a1te, a2te, a3te, wie, wce, woe, ue, ve, ape, 8, OE,
+            lambda: [halo(2, ape, 8, 8, True, 0), halo(3, ape, 8, 8, False, 0)], 1, fin_e)
+    cot_load = pltpu.make_async_copy(cot_h, cot, in_sem.at[7])
+    cot_load.start()
+    def fin_d(t, c0, cn):
+        c = pl.ds(c0, cn)
+        obuf[:, c] = (mid[:, c] + (t + gd_ref[2:3, c])).astype(BF)
+    forward(mid_rows, gd_ref, a1td, a2td, a3td, wid, wcd, wod, ud, vd, apd, 16, OD,
+            lambda: [halo(4, apd, 16, 16, True, 0)], 4, fin_d)
+    ocopy = pltpu.make_async_copy(obuf, out_h, o_sem.at[0])
+    ocopy.start()
+
+    used = [0, 0]
+    def wgrad(at, rhs, dst, row0, which, step):
+        st = (st8, st16)[which]
+        m = at.shape[0]
+        for i in range(m // step):
+            k = used[which]; slot = k % 2
+            c = pltpu.make_async_copy(st.at[slot], dst.at[pl.ds(row0 + i * step, step)], g_sem.at[which, slot])
+            if k >= 2: c.wait()
+            st[slot] = jnp.dot(at[i * step:(i + 1) * step, :], rhs, preferred_element_type=F32).astype(BF)
+            c.start()
+            used[which] += 1
+
+    def back_norm(src, grad, par, row, accum, width, emit, step=128):
+        g, s = par[row:row + 1, 0:width], par[row + 1:row + 2, 0:width]
+        accum[...] = jnp.zeros_like(accum)
+        def body(r):
+            n, f = norm_of(src(r, step))
+            h = n * g + s
+            gh = grad[pl.ds(r, step), 0:width] * slope(h)
+            accum[0] += fold8(gh * n)
+            accum[1] += fold8(gh)
+            p = gh * g
+            m1 = jnp.mean(p, axis=-1, keepdims=True)
+            m2 = jnp.mean(p * n, axis=-1, keepdims=True)
+            emit(r, step, f * (p - m1 - n * m2))
+        row_loop(step, body)
+
+    def small(row, acc, width):
+        small_ref[row:row + 1, 0:width] = jnp.sum(acc[0], axis=0, keepdims=True)
+        small_ref[row + 1:row + 2, 0:width] = jnp.sum(acc[1], axis=0, keepdims=True)
+
+    def backward(gy, par, sb, x_of, a1t, a2t, a3t, wi, wc, wo, u, v, gp, lead, offsets, hal, gi, gc, go, finish, load_x=None):
+        accb[...] = jnp.zeros_like(accb)
+        def bsum(r): accb[...] += fold8(gy[pl.ds(r, 32), :].astype(F32))
+        row_loop(32, bsum)
+        small_ref[sb + 2:sb + 3, :] = jnp.sum(accb[...], axis=0, keepdims=True)
+        mm_t(gy, wo, big)
+        wgrad(a3t, gy[...], go, 0, 1, 160)
+        def keep(r, n, val): into(gp, lead)(r, n, val.astype(BF))
+        back_norm(lambda r, n: v[pl.ds(r, n), :], big, par, 5, acc3, N_, keep)
+        hs = hal()
+        small(sb + 5, acc3, N_)
+        for h in hs: halo_wait(h)
+        stack(gp, lead, [-o for o in offsets])
+        for k in range(len(offsets)): wgrad(a2t, lk[k], gc, k * N_, 0, 400)
+        mm_taps_t(lk, wc, big, len(offsets))
+        def keep2(r, n, val): gub[pl.ds(r, n), :] = val.astype(BF)
+        back_norm(lambda r, n: u[pl.ds(r, n), :], big, par, 3, acc2, N_, keep2)
+        small(sb + 3, acc2, N_)
+        wgrad(a1t, gub[...], gi, 0, 0, 400)
+        mm_t(gub, wi, big)
+        if load_x is not None: load_x.wait()
+        back_norm(x_of, big, par, 0, acc1, W, finish)
+        small(sb, acc1, W)
+
+    cot_load.wait()
+    ocopy.wait()
+    def fin_mid(r, n, val):
+        g = cot[pl.ds(r, n), :].astype(F32) + val
+        mid[pl.ds(r, n), :] = g
+        obuf[pl.ds(r, n), :] = g.astype(BF)
+    small_ref[...] = jnp.zeros_like(small_ref)
+    backward(cot, gd_ref, 8, mid_rows, a1td, a2td, a3td, wid, wcd, wod, ud, vd, gpd, 0, OD,
+             lambda: [halo(5, gpd, 0, 16, False, 0)], gid_h, gcd_h, god_h, fin_mid)
+    tok_load = pltpu.make_async_copy(tok_h, tok, in_sem.at[7])
+    tok_load.start()
+    def fin_tok(r, n, val):
+        mid[pl.ds(r, n), :] = mid[pl.ds(r, n), :] + val
+    backward(obuf, ge_ref, 0, tok_rows, a1te, a2te, a3te, wie, wce, woe, ue, ve, gpe, 8, OE,
+             lambda: [halo(6, gpe, 8, 8, True, 0), halo(7, gpe, 8, 8, False, 0)], gie_h, gce_h, goe_h, fin_tok, tok_load)
+    tcopy = pltpu.make_async_copy(mid, tg_h, o_sem.at[1])
+    tcopy.start()
+    for which, (st, dst) in enumerate(((st8, gie_h), (st16, goe_h))):
+        for slot in range(2):
+            pltpu.make_async_copy(st.at[slot], dst.at[pl.ds(0, st.shape[1])], g_sem.at[which, slot]).wait()
+    tcopy.wait()
+
+def compute(tok, cot, ids, ge, gd, weights, cid=2):
+    V = pltpu.VMEM
+    any_ = pl.BlockSpec(memory_space=pl.ANY)
+    vm = pl.BlockSpec(memory_space=pltpu.VMEM)
+    sd = jax.ShapeDtypeStruct
+    wshape = [(W, N_), (5 * N_, N_), (N_, W), (W, N_), (3 * N_, N_), (N_, W)]
+    big_shape = [V(s, BF) for s in wshape]
+    tbuf_alias = None
+    scratch = big_shape + [V((ROWS, W), BF), V((ROWS, W), F32)] + [V((ROWS, N_), F32)] * 4 + [
+        V((ROWS, W), BF), V((ROWS, N_), BF), V((W, ROWS), BF), V((W, ROWS), BF)] + [V((N_, ROWS), BF)] * 4 + [
+        V((2, 272, N_), F32), V((2, 272, N_), F32), V((2, 272, N_), F32), V((2, 288, 128), jnp.int32),
+        V((5, ROWS, N_), BF), V((ROWS, W), F32), V((2, 400, N_), BF), V((2, 160, W), BF),
+        V((2, 8, W), F32), V((2, 8, N_), F32), V((2, 8, N_), F32), V((8, W), F32),
+        pltpu.SemaphoreType.DMA((8,)), pltpu.SemaphoreType.DMA((8,)), pltpu.SemaphoreType.DMA((8,)), pltpu.SemaphoreType.DMA((2, 2)), pltpu.SemaphoreType.DMA((2,))]
+    return pl.pallas_call(
+        comp_kernel,
+        out_shape=[sd((ROWS, W), BF), sd((ROWS, W), F32), sd((16, W), F32)] + [sd(s, BF) for s in wshape],
+        in_specs=[any_, any_, vm, vm, vm] + [any_] * 6,
+        out_specs=[any_, any_, vm] + [any_] * 6,
+        scratch_shapes=scratch,
+        compiler_params=pltpu.CompilerParams(collective_id=cid, has_side_effects=True, vmem_limit_bytes=63 * 2**20),
+    )(tok, cot, ids, ge, gd, *weights)
+
+
 def per_device(
-    tokens,
-    doc_ids,
-    cotangent,
-    enc_in,
-    enc_conv,
-    enc_out,
-    enc_gain,
-    enc_shift,
-    enc_bias,
-    dec_in,
-    dec_conv,
-    dec_out,
-    dec_gain,
-    dec_shift,
-    dec_bias,
+    tokens, doc_ids, cotangent, enc_in, enc_conv, enc_out, enc_gain, enc_shift, enc_bias,
+    dec_in, dec_conv, dec_out, dec_gain, dec_shift, dec_bias,
 ):
+    flat = [enc_in, enc_conv, enc_out, dec_in, dec_conv, dec_out]
+    size = lax.axis_size("dp"), lax.axis_size("seq"), tokens.shape
+    if size != (8, 4, (2, 1, LEN_, W)):
+        return any_mesh(
+            tokens, doc_ids, cotangent, flat, (enc_gain, enc_shift, enc_bias), (dec_gain, dec_shift, dec_bias)
+        )
+    order = lambda k, t: t + k * 0.01
+    weights = gather([w.reshape(n, L) for w, (n, L, _) in zip(flat, MATS)], order)
+    ids = jnp.broadcast_to(doc_ids.reshape(2, LEN_, 1), (2, LEN_, 128))
+    res = compute(
+        tokens.reshape(ROWS, W), cotangent.reshape(ROWS, W), ids,
+        table(enc_gain, enc_shift, enc_bias), table(dec_gain, dec_shift, dec_bias), weights,
+    )
+    sums = scatter(res[2], res[3:], lambda k, t: t + k)
+    s, w = sums[0], [g.reshape(-1) for g in sums[1:]]
+    e, d = untable(s[0:8]), untable(s[8:16])
+    return (
+        res[0].reshape(tokens.shape), res[1].reshape(tokens.shape), w[0], w[1], w[2], *e, w[3], w[4], w[5], *d,
+    )
+
+
+def table(gain, shift, bias):
+    def wide(v): return jnp.pad(v, (0, W - v.shape[0]))
+    one, two, three = slice(0, W), slice(W, W + N_), slice(W + N_, W + 2 * N_)
+    rows = [gain[one], shift[one], bias, wide(gain[two]), wide(shift[two]), wide(gain[three]), wide(shift[three]), jnp.zeros((W,), F32)]
+    return jnp.stack(rows)
+
+
+def untable(s):
+    gain = jnp.concatenate([s[0], s[3, :N_], s[5, :N_]])
+    shift = jnp.concatenate([s[1], s[4, :N_], s[6, :N_]])
+    return gain, shift, s[2]
+
+
+def any_mesh(tokens, doc_ids, cotangent, flat, enc_small, dec_small):
     micro_count, seqs_here, length, wide_dim = tokens.shape
-    segment_leading = max(
-        ENCODER_SPACING * ((ENCODER_TAPS - 1) // 2), DECODER_SPACING * (DECODER_TAPS - 1)
-    )
-    outputs = []
-    grads_in = []
-    weight_sums = None
-    small_sums = None
-    for batch_index in range(micro_count):
-        seg_pad = extended(doc_ids[batch_index], (("seq", 1),), segment_leading)
-        enc_weights = fetch_forward(enc_in, enc_conv, enc_out)
-        start_rows = tokens[batch_index].astype(jnp.float32)
-        middle, enc_kept = block_forward(
-            start_rows, seg_pad, segment_leading, enc_weights, enc_gain, enc_shift, enc_bias, False
-        )
-        dec_weights = fetch_forward(dec_in, dec_conv, dec_out)
-        final_rows, dec_kept = block_forward(
-            middle, seg_pad, segment_leading, dec_weights, dec_gain, dec_shift, dec_bias, True
-        )
-        outputs.append(final_rows.astype(jnp.bfloat16))
-        grad_final = cotangent[batch_index].astype(jnp.float32).reshape(-1, wide_dim)
-        dec_weights = fetch_backward(dec_in, dec_conv, dec_out)
-        grad_middle, dec_wgrads, dec_small = block_backward(
-            grad_final,
-            dec_kept,
-            seg_pad,
-            segment_leading,
-            dec_weights,
-            dec_gain,
-            True,
-            seqs_here,
-            length,
-        )
-        enc_weights = fetch_backward(enc_in, enc_conv, enc_out)
-        grad_start, enc_wgrads, enc_small = block_backward(
-            grad_middle,
-            enc_kept,
-            seg_pad,
-            segment_leading,
-            enc_weights,
-            enc_gain,
-            False,
-            seqs_here,
-            length,
-        )
-        grads_in.append(grad_start.reshape(seqs_here, length, wide_dim))
-        batch_weights = enc_wgrads + dec_wgrads
-        batch_small = enc_small + dec_small
-        if batch_index == 0:
-            weight_sums = batch_weights
-            small_sums = batch_small
-        else:
-            weight_sums = jax.tree.map(jnp.add, weight_sums, batch_weights)
-            small_sums = jax.tree.map(jnp.add, small_sums, batch_small)
-    in_shards = (
-        lax.psum_scatter(weight_sums[0], ("dp", "seq"), scatter_dimension=0, tiled=True),
-        lax.psum_scatter(weight_sums[3], ("dp", "seq"), scatter_dimension=0, tiled=True),
-    )
-    conv_shards = (
-        lax.psum_scatter(weight_sums[1], ("dp", "seq"), scatter_dimension=0, tiled=True),
-        lax.psum_scatter(weight_sums[4], ("dp", "seq"), scatter_dimension=0, tiled=True),
-    )
-    out_shards = (
-        lax.psum_scatter(weight_sums[2], ("dp", "seq"), scatter_dimension=0, tiled=True),
-        lax.psum_scatter(weight_sums[5], ("dp", "seq"), scatter_dimension=0, tiled=True),
-    )
-    small_total = lax.psum(
-        (small_sums[0], small_sums[1], small_sums[2], small_sums[3], small_sums[4], small_sums[5]),
-        ("dp", "seq"),
-    )
-    output = jnp.stack(outputs)
-    token_grad = jnp.stack(grads_in)
+    count = micro_count * seqs_here
+    lead = max(ENCODER_SPACING * ((ENCODER_TAPS - 1) // 2), DECODER_SPACING * (DECODER_TAPS - 1))
+    seg_pad = extended(doc_ids.reshape(count, length), (("seq", 1),), lead)
+    whole = [lax.all_gather(w, ("dp", "seq"), axis=0, tiled=True) for w in flat]
+    enc, dec = [
+        (whole[i].reshape(D2, D), whole[i + 1].reshape(-1, D), whole[i + 2].reshape(D, D2)) for i in (0, 3)
+    ]
+    rows = tokens.astype(jnp.float32).reshape(count, length, wide_dim)
+    middle, enc_kept = block_forward(rows, seg_pad, lead, enc, *enc_small, False)
+    final_rows, dec_kept = block_forward(middle, seg_pad, lead, dec, *dec_small, True)
+    output = final_rows.astype(jnp.bfloat16).reshape(tokens.shape)
+    grad_final = cotangent.astype(jnp.float32).reshape(-1, wide_dim)
+    grad_middle, dec_w, dec_s = block_backward(
+        grad_final, dec_kept, seg_pad, lead, dec, dec_small[0], True, count, length
+    )
+    grad_start, enc_w, enc_s = block_backward(
+        grad_middle, enc_kept, seg_pad, lead, enc, enc_small[0], False, count, length
+    )
+    w = [lax.psum_scatter(g.reshape(-1), ("dp", "seq"), scatter_dimension=0, tiled=True) for g in enc_w + dec_w]
+    s = lax.psum(enc_s + dec_s, ("dp", "seq"))
     return (
-        output,
-        token_grad,
-        in_shards[0],
-        conv_shards[0],
-        out_shards[0],
-        small_total[0],
-        small_total[1],
-        small_total[2],
-        in_shards[1],
-        conv_shards[1],
-        out_shards[1],
-        small_total[3],
-        small_total[4],
-        small_total[5],
+        output, grad_start.reshape(tokens.shape), w[0], w[1], w[2], s[0], s[1], s[2],
+        w[3], w[4], w[5], s[3], s[4], s[5],
     )
 
 

time: 1330 us -> 454 us (0.34)
  waiting for transfers between devices: 857 us -> 0 us
  Pallas kernels: 0 us -> 388 us
  local copies, waits for them, and re-layouts: 219 us -> 59 us
  matrix products: 105 us -> 0 us
  starting transfers between devices: 45.7 us -> 0 us
  blocking collectives: 44.4 us -> 0 us
  other arithmetic: 28.2 us -> 0 us
  between operations: 17 us -> 0.98 us
    unnamed x4 -> x0, waiting for transfers between devices: 855 us -> none
    pallas_call x0 -> x3, Pallas kernels: none -> 388 us  [the longest x1 154 us: scatter(): pl.pallas_call(functools.partial(scatter_kernel, order), out_shape=[jax.S...]
    dot_general x36 -> x0, matrix products: 105 us -> none  [the longest x4 17.9 us: block_backward(): jnp.einsum('nkj,kij->ni', back_stack, convolution_weight.reshape(len(shif...]
    add x10 -> x0, local copies, waits for them, and re-layouts: 98 us -> none  [per_device(): weight_sums = jax.tree.map(jnp.add, weight_sums, batch_weights)]
    ppermute x16 -> x0, starting transfers between devices: 45.6 us -> none  [the longest x6 27.2 us: extended(): before = lax.ppermute(last, axis, up)]
    psum x1 -> x0, blocking collectives: 44.4 us -> none  [per_device(): lax.psum((small_sums[0], small_sums[1], small_sums[2], small_sums[3], sma...]
    reshape x6 -> x12, local copies, waits for them, and re-layouts: 49.5 us -> 17.4 us  [the longest x6 10.9 us: per_device(): s, w = (sums[0], [g.reshape(-1) for g in sums[1:]])]
    another operation x2 -> x17, local copies, waits for them, and re-layouts: 24.5 us -> 2.91 us  [the longest x16 2.91 us: table(): return jnp.stack(rows)]
  transfers between devices with their start and end apart: 18 -> 0, of which waited for: 3 -> 0; matrix products, arithmetic and copies ran while one was open for 17% -> 0% of each run, Pallas kernels for 0% -> 0%
where the time goes in v1:
time: 454 us; the launch traced here: 448 us
  Pallas kernels  388 us (85%)
  local copies, waits for them, and re-layouts  59 us (13%)
    pallas_call x1, Pallas kernels, scatter(): pl.pallas_call(functools.partial(scatter_kernel, order), out_shape=[jax.S...  154 us
    pallas_call x1, Pallas kernels, compute(): pl.pallas_call(comp_kernel, out_shape=[sd((ROWS, W), BF), sd((ROWS, W), F...  126 us
    pallas_call x1, Pallas kernels, gather(): pl.pallas_call(functools.partial(gather_kernel, order), out_shape=[jax.Sh...  108 us
    unnamed x19, local copies, waits for them, and re-layouts  26.3 us
    reshape x6, local copies, waits for them, and re-layouts, per_device(): s, w = (sums[0], [g.reshape(-1) for g in sums[1:]])  10.9 us

profile of v1, /device:TPU:0, one launch (start us, length us, event | category | flops | bytes accessed | tf_op | source)
XLA Modules:
  0.0 447.6 jit_solution(3403098972253338475)
XLA Ops:
  10.7 1.1 reshape.80.refs_0_
  11.7 1.1 reshape.83.refs_3_
  14.8 1.1 reshape.84.refs_4_
  15.9 1.3 reshape.81.refs_1_
  18.0 2.5 copy.33
  20.5 3.6 copy.34
  24.1 107.7 %shard_map.254 = (bf16[1600,800]{1,0:T(8,128)(2,1)S(1)}, bf16[4000,800]{1,0:T(8,128)(2,1)S(1)}, bf16[800,1600]{1,0:T(8,128)(2,1)S(1)}, bf16[1600,800]{1,0:T(8,12...) custom-call(bf16[50,800]{1,0:T(8,128)(2,1)S(1)} %reshape.80.refs_0_, ...), custom_call_target="tpu_custom_call" | custom-call | tf_op jit(solution)/shard_map/pallas_call | solution.py:377
  131.8 2.9 copy-done
  134.8 2.0 copy-done.1
  136.8 1.6 copy-done.2
  138.4 1.6 copy-done.3
  139.9 1.5 copy-done.4
  141.5 1.5 copy-done.5
  142.9 125.6 %shard_map.255 = (bf16[512,1600]{1,0:T(8,128)(2,1)}, f32[512,1600]{1,0:T(8,128)}, f32[16,1600]{1,0:T(8,128)}, bf16[1600,800]{1,0:T(8,128)(2,1)}, bf16[4000,800]{...) custom-call(bf16[512,1600]{1,0:T(8,128)(2,1)} %bitcast.7, ...), custom_call_target="tpu_custom_call" | custom-call | tf_op jit(solution)/shard_map/pallas_call | solution.py:872
  268.6 3.6 copy.35
  272.2 4.7 %copy.36 = f32[2,1,256,1600]{2,3,1,0:T(8,128)} copy(f32[2,1,256,1600]{3,2,0,1:T(8,128)} %bitcast.9) | data formatting | bytes 6553600
  276.9 154.2 %shard_map.256 = (f32[16,1600]{1,0:T(8,128)}, f32[50,800]{1,0:T(8,128)}, f32[125,800]{1,0:T(8,128)}, f32[25,1600]{1,0:T(8,128)}, f32[50,800]{1,0:T(8,128)}, /*index=5*/f32[75,800]{1,0:T(8,128)}, f32[25,1600]{1,0:T(8,128)}) custom-call(f32[16,1600]{1,0:T(8,128)} %get-tuple-element.44.refs_0_, bf16[1600,800]{1,0:T(8,128)(2,1)} %get-tuple-element.45.refs_1_, ...), custom_call_target="tpu_custom_call" | custom-call | tf_op jit(solution)/shard_map/pallas_call | solution.py:565
  431.1 1.7 reshape.88
  433.9 1.7 slice_reduce_fusion
  438.3 1.7 reshape.90
  440.0 1.7 reshape.91
  441.7 1.7 reshape.93
  443.4 1.9 reshape.92
  445.3 2.1 reshape.89
  (50 shorter events, 16.5 us)
Async XLA Ops:
  0.6 17.4 %copy-start.6 = (bf16[2,1,256,1600]{2,3,1,0:T(8,128)(2,1)S(1)}, bf16[2,1,256,1600]{2,3,1,0:T(8,128)(2,1)}, u32[]{:S(2)}) copy-start(bf16[2,1,256,1600]{2,3,1,0:T(8,128)(2,1)} %param.15) | copy-start | bytes 4915204
  131.8 2.9 copy-start
  134.8 2.0 copy-start.1
  136.8 1.6 copy-start.2
  138.4 1.6 copy-start.3
  139.9 1.5 copy-start.4
  141.5 1.5 copy-start.5
